TPU v7x, 32 devices: a whole 2x2x4 slice. The times are simulated.
32 devices in a mesh: rep: 4 (over x, core), shard: 8 (over z, y).
Axes of the slice: x: 2, y: 2, z: 4, core: 2. Of those that a mesh axis runs over, the one named last changes fastest.
Arguments:
- tokens: bfloat16 [8192, 1024], P(('rep', 'shard')), may hold values from -6 to 6
- norm_attn: bfloat16 [1024], P('shard'), may hold values from 0.099609375 to 1.8984375
- w_query: bfloat16 [1024, 1024], P('shard'), may hold values from -0.375 to 0.375
- w_latent: bfloat16 [1024, 512], P('shard'), may hold values from -0.1875 to 0.1875
- w_key_up: bfloat16 [2, 256, 512], P(None, 'shard'), may hold values from -0.375 to 0.375
- w_value_up: bfloat16 [2, 256, 512], P(None, 'shard'), may hold values from -0.375 to 0.375
- w_out: bfloat16 [1024, 1024], P(None, 'shard'), may hold values from -0.75 to 0.75
- norm_ffn: bfloat16 [1024], P('shard'), may hold values from 0.099609375 to 1.8984375
- w_gate: bfloat16 [1024, 2816], P('shard'), may hold values from -0.1875 to 0.1875
- w_up: bfloat16 [1024, 2816], P('shard'), may hold values from -0.1875 to 0.1875
- w_down: bfloat16 [2816, 1024], P('shard'), may hold values from -0.109375 to 0.109375
- cotangent: bfloat16 [8192, 1024], P(('rep', 'shard')), may hold values from -6 to 6
Outputs:
- output: bfloat16 [8192, 1024], P(('rep', 'shard'))
- grad_tokens: bfloat16 [8192, 1024], P(('rep', 'shard'))
- grad_norm_attn: float32 [1024], P('shard')
- grad_w_query: float32 [1024, 1024], P('shard')
- grad_w_latent: float32 [1024, 512], P('shard')
- grad_w_key_up: float32 [2, 256, 512], P(None, 'shard')
- grad_w_value_up: float32 [2, 256, 512], P(None, 'shard')
- grad_w_out: float32 [1024, 1024], P(None, 'shard')
- grad_norm_ffn: float32 [1024], P('shard')
- grad_w_gate: float32 [1024, 2816], P('shard')
- grad_w_up: float32 [1024, 2816], P('shard')
- grad_w_down: float32 [2816, 1024], P('shard')
All inputs are finite; a program needn't handle non-finite values.
Results may differ from a plain program's by a relative error of at most 0.018.
Values may be sent and summed in bfloat16 or wider, within the bound.
No kernel may reach another device: no remote copies, remote signals or barrier semaphores. Data moves between devices by JAX's collectives and lax.ppermute only.
A program may use at most 192 MiB of HBM per device.

v0:
```python
import jax
import jax.numpy as jnp
from jax import lax
from jax.sharding import PartitionSpec as P

HQ = 16
HD = 64
LG = 2
LAT = 256


epsilon = 1e-05


def rms_scale(rows_in):
    return lax.rsqrt(jnp.mean(rows_in * rows_in, axis=-1, keepdims=True) + epsilon)


def outer_sum(left, right):
    return lax.dot_general(
        left, right, (((0,), (0,)), ((), ())), preferred_element_type=jnp.float32
    )


def back_dot(left, weight):
    return lax.dot_general(
        left, weight, (((1,), (1,)), ((), ())), preferred_element_type=jnp.float32
    )


def expand(latents, up_weight):
    length = latents.shape[0]
    grouped = latents.reshape(length, LG, LAT)
    projected = jnp.einsum("tgl,glk->tgk", grouped, up_weight, preferred_element_type=jnp.float32)
    return projected.astype(jnp.bfloat16).reshape(length, HQ, HD)


def score_block(query_heads, key_heads):
    length = query_heads.shape[0]
    scores = jnp.einsum(
        "qhd,khd->hqk", query_heads, key_heads, preferred_element_type=jnp.float32
    ) * HD ** (-0.5)
    row_ids = lax.broadcasted_iota(jnp.int32, (length, length), 0)
    col_ids = lax.broadcasted_iota(jnp.int32, (length, length), 1)
    return jnp.where(col_ids <= row_ids, scores, -1e30)


def shards(
    tokens,
    norm_attn,
    w_query,
    w_latent,
    w_key_up,
    w_value_up,
    w_out,
    norm_ffn,
    w_gate,
    w_up,
    w_down,
    cotangent,
):
    gathered = (
        lax.all_gather(norm_attn, "shard", axis=0, tiled=True),
        lax.all_gather(w_query, "shard", axis=0, tiled=True),
        lax.all_gather(w_latent, "shard", axis=0, tiled=True),
        lax.all_gather(w_key_up, "shard", axis=1, tiled=True),
        lax.all_gather(w_value_up, "shard", axis=1, tiled=True),
        lax.all_gather(w_out, "shard", axis=1, tiled=True),
        lax.all_gather(norm_ffn, "shard", axis=0, tiled=True),
        lax.all_gather(w_gate, "shard", axis=0, tiled=True),
        lax.all_gather(w_up, "shard", axis=0, tiled=True),
        lax.all_gather(w_down, "shard", axis=0, tiled=True),
    )
    (
        gain_attn,
        query_full,
        latent_full,
        key_full,
        value_full,
        out_full,
        gain_ffn,
        gate_full,
        up_full,
        down_full,
    ) = gathered
    inputs = tokens.astype(jnp.float32)
    length = inputs.shape[0]
    scale_attn = rms_scale(inputs)
    normed_attn = (inputs * scale_attn * gain_attn.astype(jnp.float32)).astype(jnp.bfloat16)
    queries = jnp.dot(normed_attn, query_full, preferred_element_type=jnp.float32).astype(
        jnp.bfloat16
    )
    latents = jnp.dot(normed_attn, latent_full, preferred_element_type=jnp.float32).astype(
        jnp.bfloat16
    )
    query_heads = queries.reshape(length, HQ, HD)
    key_heads = expand(latents, key_full)
    value_heads = expand(latents, value_full)
    scores = score_block(query_heads, key_heads)
    maxima = jnp.max(scores, axis=-1, keepdims=True)
    log_total = maxima + jnp.log(jnp.sum(jnp.exp(scores - maxima), axis=-1, keepdims=True))
    attn_probs = jnp.exp(scores - log_total).astype(jnp.bfloat16)
    mixed_heads = jnp.einsum(
        "hqk,khd->qhd", attn_probs, value_heads, preferred_element_type=jnp.float32
    )
    mixed_heads = mixed_heads.astype(jnp.bfloat16).reshape(length, HQ * HD)
    residual = inputs + jnp.dot(mixed_heads, out_full, preferred_element_type=jnp.float32)
    scale_ffn = rms_scale(residual)
    normed_ffn = (residual * scale_ffn * gain_ffn.astype(jnp.float32)).astype(jnp.bfloat16)
    gate_proj = jnp.dot(normed_ffn, gate_full, preferred_element_type=jnp.float32)
    up_proj = jnp.dot(normed_ffn, up_full, preferred_element_type=jnp.float32)
    sigmoid_gate = jax.nn.sigmoid(gate_proj)
    silu_gate = gate_proj * sigmoid_gate
    activated = (silu_gate * up_proj).astype(jnp.bfloat16)
    output = (residual + jnp.dot(activated, down_full, preferred_element_type=jnp.float32)).astype(
        jnp.bfloat16
    )
    weights_back = (
        lax.all_gather(norm_attn, "shard", axis=0, tiled=True),
        lax.all_gather(w_query, "shard", axis=0, tiled=True),
        lax.all_gather(w_latent, "shard", axis=0, tiled=True),
        lax.all_gather(w_key_up, "shard", axis=1, tiled=True),
        lax.all_gather(w_value_up, "shard", axis=1, tiled=True),
        lax.all_gather(w_out, "shard", axis=1, tiled=True),
        lax.all_gather(norm_ffn, "shard", axis=0, tiled=True),
        lax.all_gather(w_gate, "shard", axis=0, tiled=True),
        lax.all_gather(w_up, "shard", axis=0, tiled=True),
        lax.all_gather(w_down, "shard", axis=0, tiled=True),
    )
    gain_attn_b, query_b, latent_b, key_b, value_b, out_b, gain_ffn_b, gate_b, up_b, down_b = (
        weights_back
    )
    grad_out = cotangent.astype(jnp.float32)
    grad_w_down = outer_sum(activated, cotangent)
    grad_act = back_dot(cotangent, down_b)
    grad_gate = (
        grad_act * up_proj * sigmoid_gate * (1.0 + gate_proj * (1.0 - sigmoid_gate))
    ).astype(jnp.bfloat16)
    grad_up_proj = (grad_act * silu_gate).astype(jnp.bfloat16)
    grad_w_gate = outer_sum(normed_ffn, grad_gate)
    grad_w_up = outer_sum(normed_ffn, grad_up_proj)
    grad_normed_ffn = back_dot(grad_gate, gate_b) + back_dot(grad_up_proj, up_b)
    grad_norm_ffn = jnp.sum(grad_normed_ffn * residual * scale_ffn, axis=0)
    weighted_ffn = grad_normed_ffn * gain_ffn_b.astype(jnp.float32)
    grad_residual = (
        grad_out
        + scale_ffn * weighted_ffn
        - residual * scale_ffn**3 * jnp.mean(weighted_ffn * residual, axis=-1, keepdims=True)
    )
    grad_attn = grad_residual.astype(jnp.bfloat16)
    grad_w_out = outer_sum(mixed_heads, grad_attn)
    grad_mixed = back_dot(grad_attn, out_b).astype(jnp.bfloat16).reshape(length, HQ, HD)
    probs_again = jnp.exp(score_block(query_heads, key_heads) - log_total)
    grad_probs = jnp.einsum(
        "qhd,khd->hqk", grad_mixed, value_heads, preferred_element_type=jnp.float32
    )
    grad_scores = (
        probs_again * (grad_probs - jnp.sum(probs_again * grad_probs, axis=-1, keepdims=True))
    ).astype(jnp.bfloat16)
    grad_heads_q = jnp.einsum(
        "hqk,khd->qhd", grad_scores, key_heads, preferred_element_type=jnp.float32
    ) * HD ** (-0.5)
    grad_keys = jnp.einsum(
        "hqk,qhd->khd", grad_scores, query_heads, preferred_element_type=jnp.float32
    ) * HD ** (-0.5)
    grad_values = jnp.einsum(
        "hqk,qhd->khd",
        probs_again.astype(jnp.bfloat16),
        grad_mixed,
        preferred_element_type=jnp.float32,
    )
    grad_queries = grad_heads_q.astype(jnp.bfloat16).reshape(length, HQ * HD)
    grad_keys = grad_keys.astype(jnp.bfloat16).reshape(length, LG, HQ * HD // LG)
    grad_values = grad_values.astype(jnp.bfloat16).reshape(length, LG, HQ * HD // LG)
    grouped = latents.reshape(length, LG, LAT)
    grad_w_key_up = jnp.einsum(
        "tgl,tgk->glk", grouped, grad_keys, preferred_element_type=jnp.float32
    )
    grad_w_value_up = jnp.einsum(
        "tgl,tgk->glk", grouped, grad_values, preferred_element_type=jnp.float32
    )
    grad_latents = jnp.einsum("tgk,glk->tgl", grad_keys, key_b, preferred_element_type=jnp.float32)
    grad_latents = grad_latents + jnp.einsum(
        "tgk,glk->tgl", grad_values, value_b, preferred_element_type=jnp.float32
    )
    grad_latents = grad_latents.reshape(length, LG * LAT).astype(jnp.bfloat16)
    grad_w_query = outer_sum(normed_attn, grad_queries)
    grad_w_latent = outer_sum(normed_attn, grad_latents)
    grad_normed_attn = back_dot(grad_queries, query_b) + back_dot(grad_latents, latent_b)
    grad_norm_attn = jnp.sum(grad_normed_attn * inputs * scale_attn, axis=0)
    weighted_attn = grad_normed_attn * gain_attn_b.astype(jnp.float32)
    grad_tokens = (
        grad_residual
        + scale_attn * weighted_attn
        - inputs * scale_attn**3 * jnp.mean(weighted_attn * inputs, axis=-1, keepdims=True)
    )
    grad_tokens = grad_tokens.astype(jnp.bfloat16)
    group_sums = (
        lax.psum_scatter(grad_norm_attn, "shard", scatter_dimension=0, tiled=True),
        lax.psum_scatter(grad_w_query, "shard", scatter_dimension=0, tiled=True),
        lax.psum_scatter(grad_w_latent, "shard", scatter_dimension=0, tiled=True),
        lax.psum_scatter(grad_w_key_up, "shard", scatter_dimension=1, tiled=True),
        lax.psum_scatter(grad_w_value_up, "shard", scatter_dimension=1, tiled=True),
        lax.psum_scatter(grad_w_out, "shard", scatter_dimension=1, tiled=True),
        lax.psum_scatter(grad_norm_ffn, "shard", scatter_dimension=0, tiled=True),
        lax.psum_scatter(grad_w_gate, "shard", scatter_dimension=0, tiled=True),
        lax.psum_scatter(grad_w_up, "shard", scatter_dimension=0, tiled=True),
        lax.psum_scatter(grad_w_down, "shard", scatter_dimension=0, tiled=True),
    )
    summed = (
        lax.psum(group_sums[0].astype(jnp.bfloat16), "rep").astype(jnp.float32),
        lax.psum(group_sums[1].astype(jnp.bfloat16), "rep").astype(jnp.float32),
        lax.psum(group_sums[2].astype(jnp.bfloat16), "rep").astype(jnp.float32),
        lax.psum(group_sums[3].astype(jnp.bfloat16), "rep").astype(jnp.float32),
        lax.psum(group_sums[4].astype(jnp.bfloat16), "rep").astype(jnp.float32),
        lax.psum(group_sums[5].astype(jnp.bfloat16), "rep").astype(jnp.float32),
        lax.psum(group_sums[6].astype(jnp.bfloat16), "rep").astype(jnp.float32),
        lax.psum(group_sums[7].astype(jnp.bfloat16), "rep").astype(jnp.float32),
        lax.psum(group_sums[8].astype(jnp.bfloat16), "rep").astype(jnp.float32),
        lax.psum(group_sums[9].astype(jnp.bfloat16), "rep").astype(jnp.float32),
    )
    return (
        output,
        grad_tokens,
        summed[0],
        summed[1],
        summed[2],
        summed[3],
        summed[4],
        summed[5],
        summed[6],
        summed[7],
        summed[8],
        summed[9],
    )


def solution(mesh):
    return jax.shard_map(
        shards,
        mesh=mesh,
        in_specs=(
            P(("rep", "shard"), None),
            P("shard"),
            P("shard", None),
            P("shard", None),
            P(None, "shard", None),
            P(None, "shard", None),
            P(None, "shard"),
            P("shard"),
            P("shard", None),
            P("shard", None),
            P("shard", None),
            P(("rep", "shard"), None),
        ),
        out_specs=(
            P(("rep", "shard"), None),
            P(("rep", "shard"), None),
            P("shard"),
            P("shard", None),
            P("shard", None),
            P(None, "shard", None),
            P(None, "shard", None),
            P(None, "shard"),
            P("shard"),
            P("shard", None),
            P("shard", None),
            P("shard", None),
        ),
        check_vma=False,
    )
```

profile of v0, /device:TPU:0, one launch (start us, length us, event | category | flops | bytes accessed | tf_op | source)
XLA Modules:
  0.0 1525.3 jit_solution(16579019926269672240)
XLA Ops:
  11.2 22.3 %all-gather = bf16[8,1,128]{2,1,0:T(2,128)(2,1)S(1)} all-gather(bf16[1,1,128]{2,1,0:T(2,128)(2,1)} %bitcast.110), channel_id=1, replica_groups=mesh['rep'=4,'shard'=8] {'shard'}, dimensions={0}, use_global_device_ids=true | all-gather | bytes 2304 | tf_op jit(solution)/shard_map/all_gather | solution.py:63
  33.5 16.5 %all-gather.1 = bf16[8,1,128]{2,1,0:T(2,128)(2,1)S(1)} all-gather(bf16[1,1,128]{2,1,0:T(2,128)(2,1)} %bitcast.111), channel_id=1, replica_groups=mesh['rep'=4,'shard'=8] {'shard'}, dimensions={0}, use_global_device_ids=true | all-gather | bytes 2304 | tf_op jit(solution)/shard_map/all_gather | solution.py:69
  51.3 31.9 %all_gather.42 = bf16[2,256,512]{2,1,0:T(8,128)(2,1)S(1)} all-gather(bf16[2,32,512]{2,1,0:T(8,128)(2,1)} %param.17), channel_id=1, replica_groups=mesh['rep'=4,'shard'=8] {'shard'}, dimensions={1}, use_global_device_ids=true | all-gather | bytes 589824 | tf_op jit(solution)/shard_map/all_gather | solution.py:67
  83.2 32.4 %all_gather.44 = bf16[2,256,512]{2,1,0:T(8,128)(2,1)S(1)} all-gather(bf16[2,32,512]{2,1,0:T(8,128)(2,1)} %param.16), channel_id=1, replica_groups=mesh['rep'=4,'shard'=8] {'shard'}, dimensions={1}, use_global_device_ids=true | all-gather | bytes 589824 | tf_op jit(solution)/shard_map/all_gather | solution.py:66
  115.7 1.9 convolution_convert_fusion.6
  118.9 3.4 convolution_convert_fusion.5
  127.4 34.6 %all-gather.13.cloned.1.call-done = bf16[1024,1024]{1,0:T(8,128)(2,1)} async-done(((bf16[1024,128]{1,0:T(8,128)(2,1)}), bf16[1024,1024]{1,0:T(8,128)(2,1)}) %all-gather.13.cloned.1.call-update) | async-done | bytes 2097168 | tf_op jit(solution)/shard_map/all_gather | solution.py:68
  162.0 2.4 multiply_reduce_fusion.3
  164.6 90.3 %all-gather.15.cloned.1.call-done = bf16[1024,2816]{1,0:T(8,128)(2,1)} async-done(((bf16[128,2816]{1,0:T(8,128)(2,1)}), bf16[1024,2816]{1,0:T(8,128)(2,1)}) %all-gather.15.cloned.1.call-update) | async-done | bytes 5767184 | tf_op jit(solution)/shard_map/all_gather | solution.py:70
  254.9 5.9 fusion.33
  260.8 87.0 %all-gather.17.cloned.1.call-done = bf16[1024,2816]{1,0:T(8,128)(2,1)} async-done(((bf16[128,2816]{1,0:T(8,128)(2,1)}), bf16[1024,2816]{1,0:T(8,128)(2,1)}) %all-gather.17.cloned.1.call-update) | async-done | bytes 5767184 | tf_op jit(solution)/shard_map/all_gather | solution.py:71
  347.8 5.9 fusion.34
  353.7 87.0 %all-gather.19.cloned.1.call-done = bf16[2816,1024]{1,0:T(8,128)(2,1)} async-done(((bf16[352,1024]{1,0:T(8,128)(2,1)}), bf16[2816,1024]{1,0:T(8,128)(2,1)}) %all-gather.19.cloned.1.call-update) | async-done | bytes 5767184 | tf_op jit(solution)/shard_map/all_gather | solution.py:72
  440.7 8.2 multiply_convert_fusion.1
  448.9 5.6 fusion.35
  454.6 1.9 multiply_reduce_fusion.1
  458.9 3.8 multiply_reduce_fusion
  465.5 2.4 fusion.37
  468.0 3.4 convolution_convert_fusion.2
  476.5 1.9 fusion.27
  480.0 2.8 fusion.29
  482.9 2.8 fusion.18
  485.8 7.3 fusion.39
  493.4 7.3 fusion.40
  501.8 7.4 fusion.41
  511.1 18.6 %reduce-scatter.13.cloned.1.call-done = f32[2,32,512]{2,1,0:T(8,128)} async-done(((f32[2,256,512]{2,1,0:T(8,128)}), f32[2,32,512]{2,1,0:T(8,128)}) %reduce-scatter.13.cloned.1.call-update) | async-done | bytes 131088 | tf_op jit(solution)/shard_map/reduce_scatter | solution.py:202
  531.2 64.8 %reduce-scatter.15.cloned.1.call-done = f32[2,32,512]{2,1,0:T(8,128)} async-done(((f32[2,256,512]{2,1,0:T(8,128)}), f32[2,32,512]{2,1,0:T(8,128)}) %reduce-scatter.15.cloned.1.call-update) | async-done | bytes 131088 | tf_op jit(solution)/shard_map/reduce_scatter | solution.py:203
  597.5 69.0 %reduce-scatter.11.cloned.1.call-done = f32[128,512]{1,0:T(8,128)} async-done(((f32[1024,512]{1,0:T(8,128)}), f32[128,512]{1,0:T(8,128)}) %reduce-scatter.11.cloned.1.call-update) | async-done | bytes 262160 | tf_op jit(solution)/shard_map/reduce_scatter | solution.py:201
  668.2 88.9 %reduce-scatter.9.cloned.1.call-done = f32[128,1024]{1,0:T(8,128)} async-done(((f32[1024,1024]{1,0:T(8,128)}), f32[128,1024]{1,0:T(8,128)}) %reduce-scatter.9.cloned.1.call-update) | async-done | bytes 524304 | tf_op jit(solution)/shard_map/reduce_scatter | solution.py:200
  757.1 1.8 convert_element_type.193
  758.9 90.5 %reduce-scatter.17.cloned.1.call-done = f32[1024,128]{1,0:T(8,128)} async-done(((f32[1024,1024]{1,0:T(8,128)}), f32[1024,128]{1,0:T(8,128)}) %reduce-scatter.17.cloned.1.call-update) | async-done | bytes 524304 | tf_op jit(solution)/shard_map/reduce_scatter | solution.py:204
  849.4 1.8 convert_element_type.201
  851.2 194.2 %reduce-scatter.19.cloned.1.call-done = f32[128,2816]{1,0:T(8,128)} async-done(((f32[1024,2816]{1,0:T(8,128)}), f32[128,2816]{1,0:T(8,128)}) %reduce-scatter.19.cloned.1.call-update) | async-done | bytes 1441808 | tf_op jit(solution)/shard_map/reduce_scatter | solution.py:206
  1045.4 2.3 convert_element_type.205
  1047.7 193.1 %reduce-scatter.21.cloned.1.call-done = f32[128,2816]{1,0:T(8,128)} async-done(((f32[1024,2816]{1,0:T(8,128)}), f32[128,2816]{1,0:T(8,128)}) %reduce-scatter.21.cloned.1.call-update) | async-done | bytes 1441808 | tf_op jit(solution)/shard_map/reduce_scatter | solution.py:207
  1240.8 2.3 convert_element_type.207
  1243.1 193.0 %reduce-scatter.23.cloned.1.call-done = f32[352,1024]{1,0:T(8,128)} async-done(((f32[2816,1024]{1,0:T(8,128)}), f32[352,1024]{1,0:T(8,128)}) %reduce-scatter.23.cloned.1.call-update) | async-done | bytes 1441808 | tf_op jit(solution)/shard_map/reduce_scatter | solution.py:208
  1436.1 2.3 convert_element_type.209
  1438.5 2.3 fusion.36
  1440.8 2.9 fusion.17
  1443.7 19.7 %all-reduce.2 = (bf16[1024]{0:T(1024)(128)(2,1)S(1)}, bf16[1024]{0:T(1024)(128)(2,1)S(1)}) all-reduce(f32[1024]{0:T(1024)S(1)} %get-tuple-element.14, f32[1024]{0:T(1024)S(1)} %get-tuple-element.12), channel_id=2, replica_groups=mesh['rep'=4,'shard'=8] {'shard'}, use_global_device_ids=true, to_apply=%region_8.9.clone | all-reduce | flops 2048 | bytes 12288
  1463.6 6.6 all-reduce.3
  1471.1 2.4 fusion.14
  1473.5 5.5 fusion.3
  1479.0 26.6 %all-reduce.7.cloned.1.call-done = (bf16[128,1024]{1,0:T(8,128)(2,1)}, bf16[128,512]{1,0:T(8,128)(2,1)}, bf16[2,32,512]{2,1,0:T(8,128)(2,1)}, bf16[2,32,512]{2,1...) async-done(((bf16[128,1024]{1,0:T(8,128)(2,1)}, bf16[128,512]{1,0:T(8,128)(2,1)}, ...) | async-done | bytes 2949136 | tf_op jit(solution)/shard_map/psum | solution.py:212
  1505.7 1.9 convert_element_type.194
  1512.2 1.8 convert_element_type.202
  1514.0 2.3 convert_element_type.206
  (129 shorter events, 39.2 us)
Async XLA Ops:
  7.2 108.5 %copy-start.2 = (bf16[256,1024]{1,0:T(8,128)(2,1)S(1)}, bf16[256,1024]{1,0:T(8,128)(2,1)}, u32[]{:S(2)}) copy-start(bf16[256,1024]{1,0:T(8,128)(2,1)} %param.12) | copy-start | bytes 1572868
  7.2 108.5 %all-gather.9.cloned.1.call-start = ((), (), s32[]{:S(2)}) async-start(), calls=%async_computation.8 | async-start | bytes 1179648 | tf_op jit(solution)/shard_map/all_gather | solution.py:65
  7.9 110.9 %all-gather.11.cloned.1.call-start = ((), (), s32[]{:S(2)}) async-start(), calls=%async_computation.9 | async-start | bytes 2359296 | tf_op jit(solution)/shard_map/all_gather | solution.py:64
  8.7 153.3 %all-gather.13.cloned.1.call-start = ((), (), s32[]{:S(2)}) async-start(), calls=%async_computation.10 | async-start | bytes 2359296 | tf_op jit(solution)/shard_map/all_gather | solution.py:68
  9.4 245.5 %all-gather.15.cloned.1.call-start = ((), (), s32[]{:S(2)}) async-start(), calls=%async_computation.11 | async-start | bytes 6488064 | tf_op jit(solution)/shard_map/all_gather | solution.py:70
  10.0 337.8 %all-gather.17.cloned.1.call-start = ((), (), s32[]{:S(2)}) async-start(), calls=%async_computation.12 | async-start | bytes 6488064 | tf_op jit(solution)/shard_map/all_gather | solution.py:71
  10.6 430.1 %all-gather.19.cloned.1.call-start = ((), (), s32[]{:S(2)}) async-start(), calls=%async_computation.13 | async-start | bytes 6488064 | tf_op jit(solution)/shard_map/all_gather | solution.py:72
  11.1 518.5 %reduce-scatter.13.cloned.1.call-start = ((), (), s32[]{:S(2)}) async-start(), calls=%async_computation.16 | async-start | bytes 1179648 | tf_op jit(solution)/shard_map/reduce_scatter | solution.py:202
  115.7 11.8 copy-start.10
  118.8 5.5 copy-start.11
  123.5 1.7 copy-start.12
  124.3 2.0 copy-start
  127.4 37.0 %copy-start.20 = (bf16[16,64,256]{2,1,0:T(8,128)(2,1)}, bf16[16,64,256]{2,1,0:T(8,128)(2,1)S(1)}, u32[]{:S(2)}) copy-start(bf16[16,64,256]{2,1,0:T(8,128)(2,1)S(1)} %convolution_convert_fusion.4) | copy-start | bytes 1572868
  164.4 292.1 %copy-start.5 = (f32[256,1024]{1,0:T(8,128)}, f32[256,1024]{1,0:T(8,128)S(1)}, u32[]{:S(2)}) copy-start(f32[256,1024]{1,0:T(8,128)S(1)} %get-tuple-element.38) | copy-start | bytes 3145732
  164.6 183.2 %copy-start.8 = (bf16[256,1024]{1,0:T(8,128)(2,1)}, bf16[256,1024]{1,0:T(8,128)(2,1)S(1)}, u32[]{:S(2)}) copy-start(bf16[256,1024]{1,0:T(8,128)(2,1)S(1)} %multiply_convert_fusion.4) | copy-start | bytes 1572868
  448.9 5.6 copy-start.23
  448.9 5.6 copy-start.22
  448.9 5.6 copy-start.26
  454.6 1.9 copy-start.18
  454.6 3.3 copy-start.7
  456.9 1.0 copy-start.3
  458.8 3.9 copy-start.17
  458.8 3.9 copy-start.1
  462.7 1.2 copy-start.13
  467.9 128.1 %reduce-scatter.15.cloned.1.call-start = ((), (), s32[]{:S(2)}) async-start(), calls=%async_computation.17 | async-start | bytes 1179648 | tf_op jit(solution)/shard_map/reduce_scatter | solution.py:203
  471.4 0.8 copy-start.16
  473.5 193.0 %reduce-scatter.11.cloned.1.call-start = ((), (), s32[]{:S(2)}) async-start(), calls=%async_computation.15 | async-start | bytes 2359296 | tf_op jit(solution)/shard_map/reduce_scatter | solution.py:201
  476.5 1.9 copy-start.14
  478.4 278.7 %reduce-scatter.9.cloned.1.call-start = ((), (), s32[]{:S(2)}) async-start(), calls=%async_computation.14 | async-start | bytes 4718592 | tf_op jit(solution)/shard_map/reduce_scatter | solution.py:200
  480.0 2.9 copy-start.4
  480.0 2.9 copy-start.21
  482.9 2.9 copy-start.9
  482.9 366.5 %reduce-scatter.17.cloned.1.call-start = ((), (), s32[]{:S(2)}) async-start(), calls=%async_computation.18 | async-start | bytes 4718592 | tf_op jit(solution)/shard_map/reduce_scatter | solution.py:204
  485.8 559.6 %reduce-scatter.19.cloned.1.call-start = ((), (), s32[]{:S(2)}) async-start(), calls=%async_computation.19 | async-start | bytes 12976128 | tf_op jit(solution)/shard_map/reduce_scatter | solution.py:206
  493.2 747.6 %reduce-scatter.21.cloned.1.call-start = ((), (), s32[]{:S(2)}) async-start(), calls=%async_computation.20 | async-start | bytes 12976128 | tf_op jit(solution)/shard_map/reduce_scatter | solution.py:207
  500.7 1.0 copy-start.19
  500.8 935.3 %reduce-scatter.23.cloned.1.call-start = ((), (), s32[]{:S(2)}) async-start(), calls=%async_computation.21 | async-start | bytes 12976128 | tf_op jit(solution)/shard_map/reduce_scatter | solution.py:208
  509.2 0.7 copy-start.27
  509.2 996.5 %all-reduce.7.cloned.1.call-start = ((), (), s32[]{:S(2)}) async-start(), calls=%async_computation.22 | async-start | bytes 5898240 | tf_op jit(solution)/shard_map/psum | solution.py:212
  1243.1 197.7 %copy-start.15 = (bf16[2,256,256]{1,2,0:T(8,128)(2,1)S(1)}, bf16[2,256,256]{1,2,0:T(8,128)(2,1)}, u32[]{:S(2)}) copy-start(bf16[2,256,256]{1,2,0:T(8,128)(2,1)} %copy-done.14) | copy-start | bytes 786436
  1440.8 32.7 %copy-start.6 = (f32[256,1024]{1,0:T(8,128)S(1)}, f32[256,1024]{1,0:T(8,128)}, u32[]{:S(2)}) copy-start(f32[256,1024]{1,0:T(8,128)} %copy-done.5) | copy-start | bytes 3145732
  1505.7 10.6 copy-start.25
  1505.7 11.8 copy-start.24
Sparse Core Ops, SparseCore 0:
  10.1 42.8 all-gather.8
  55.1 54.9 all-gather.10
  112.2 49.7 all-gather.12
  164.0 90.8 all-gather.14
  256.9 90.8 all-gather.16
  349.8 90.8 all-gather.18
  468.0 61.5 reduce-scatter.12
  533.5 62.4 reduce-scatter.14
  599.5 66.9 reduce-scatter.10
  670.0 87.0 reduce-scatter.8
  761.2 88.1 reduce-scatter.16
  852.8 192.4 reduce-scatter.18
  1049.0 191.8 reduce-scatter.20
  1244.2 191.7 reduce-scatter.22
  1440.0 65.6 all-reduce.6
where the time goes:
time: 1530 us
  waiting for transfers between devices  1240 us (81%)
  blocking collectives  129 us (8%)
  matrix products  95.8 us (6%)
  other arithmetic  35.5 us (2%)
    reduce_scatter x1, waiting for transfers between devices, shards(): lax.psum_scatter(grad_w_gate, 'shard', scatter_dimension=0, tiled=True)  194 us
    reduce_scatter x1, waiting for transfers between devices, shards(): lax.psum_scatter(grad_w_up, 'shard', scatter_dimension=0, tiled=True)  193 us
    reduce_scatter x1, waiting for transfers between devices, shards(): lax.psum_scatter(grad_w_down, 'shard', scatter_dimension=0, tiled=True)  193 us
    reduce_scatter x1, waiting for transfers between devices, shards(): lax.psum_scatter(grad_w_out, 'shard', scatter_dimension=1, tiled=True)  90.5 us
    all_gather x1, waiting for transfers between devices, shards(): lax.all_gather(w_gate, 'shard', axis=0, tiled=True)  90.3 us
    reduce_scatter x1, waiting for transfers between devices, shards(): lax.psum_scatter(grad_w_query, 'shard', scatter_dimension=0, tiled=True)  88.9 us
    all_gather x1, waiting for transfers between devices, shards(): lax.all_gather(w_up, 'shard', axis=0, tiled=True)  87 us
    all_gather x1, waiting for transfers between devices, shards(): lax.all_gather(w_down, 'shard', axis=0, tiled=True)  87 us
  transfers between devices with their start and end apart: 15, of which 13 were waited for; matrix products, arithmetic and copies ran while one was open for 6% of the time, Pallas kernels for 0%

commit v1 on v0

v1 whole, which is shorter than its diff:
```python
import jax
import jax.numpy as jnp
from jax import lax
from jax.sharding import PartitionSpec as P

HQ = 16
HD = 64
LG = 2
LAT = 256
SEQ = 256
R = 4
f32 = jnp.float32
bf16 = jnp.bfloat16
epsilon = 1e-05


def rms_scale(rows_in):
    return lax.rsqrt(jnp.mean(rows_in * rows_in, axis=-1, keepdims=True) + epsilon)


def dot_nn(a, b):
    return lax.dot_general(a, b, (((1,), (0,)), ((), ())), preferred_element_type=f32)


def dot_nt(a, b):
    return lax.dot_general(a, b, (((1,), (1,)), ((), ())), preferred_element_type=f32)


def dot_tn(a, b):
    return lax.dot_general(a, b, (((0,), (0,)), ((), ())), preferred_element_type=f32)


def make_layer(mesh):
    S = mesh.shape["shard"]
    Z = S // 2
    assert mesh.shape["rep"] == R

    def flip_core(v):
        return lax.ppermute(v, "rep", [(i, i ^ 1) for i in range(R)])

    def flip_x(v):
        return lax.ppermute(v, "rep", [(i, i ^ 2) for i in range(R)])

    def flip_y(v):
        return lax.ppermute(v, "shard", [(i, i ^ 1) for i in range(S)])

    def rot_z(v, k):
        return lax.ppermute(v, "shard", [(i, (i + 2 * k) % S) for i in range(S)])

    def layer(
        tokens,
        norm_attn,
        w_query,
        w_latent,
        w_key_up,
        w_value_up,
        w_out,
        norm_ffn,
        w_gate,
        w_up,
        w_down,
        cotangent,
    ):
        r = lax.axis_index("rep")
        s = lax.axis_index("shard")
        x, c, z, y = r // 2, r % 2, s // 2, s % 2
        T, D = tokens.shape
        n_d = w_query.shape[0]
        n_l = w_key_up.shape[1]
        n_f = w_down.shape[0] // R
        q_c = w_query.shape[1] // R
        FFq = n_f * S

        def gather_rep(v):
            far = flip_x(v)
            near = flip_core(jnp.stack([v, far]))
            return jnp.stack([v, near[0], far, near[1]])

        def scatter_rep(v):
            near = flip_core(v[1::2].astype(bf16))
            chip = v[0::2] + near
            far = flip_x(chip[1].astype(bf16))
            return chip[0] + far

        def absolute(v):
            v = jnp.where(c == 1, v[jnp.array([1, 0, 3, 2])], v)
            return jnp.where(x == 1, v[jnp.array([2, 3, 0, 1])], v)

        def gather_shard(v):
            full = jnp.zeros((Z, 2) + v.shape, v.dtype)
            zeros = (0,) * v.ndim
            for k in range(Z):
                piece = v if k == 0 else rot_z(v, k)
                other = flip_y(piece)
                at = lax.rem(z - k + Z, Z)
                full = lax.dynamic_update_slice(full, piece[None, None], (at, y) + zeros)
                full = lax.dynamic_update_slice(full, other[None, None], (at, 1 - y) + zeros)
            return full.reshape((S,) + v.shape)

        def scatter_shard(v):
            v = v.reshape((Z, 2) + v.shape[1:])
            mine = lax.dynamic_index_in_dim(v, y, 1, False)
            give = lax.dynamic_index_in_dim(v, 1 - y, 1, False)
            half = (mine.astype(f32) + flip_y(give).astype(f32)).astype(bf16)
            total = lax.dynamic_index_in_dim(half, z, 0, False).astype(f32)
            for k in range(1, Z):
                piece = lax.dynamic_index_in_dim(half, lax.rem(z + k, Z), 0, False)
                total = total + rot_z(piece, k).astype(f32)
            return absolute(gather_rep(total.astype(bf16)))

        my_query = lax.dynamic_slice_in_dim(w_query, r * q_c, q_c, 1)
        my_latent = lax.dynamic_slice_in_dim(w_latent, x * LAT, LAT, 1)
        my_key = lax.dynamic_slice_in_dim(
            lax.dynamic_index_in_dim(w_key_up, x, 0, False), c * q_c, q_c, 1
        )
        my_value = lax.dynamic_slice_in_dim(
            lax.dynamic_index_in_dim(w_value_up, x, 0, False), c * q_c, q_c, 1
        )
        my_out = lax.dynamic_slice_in_dim(w_out, r * q_c, q_c, 0).T
        gains = jnp.zeros((16, q_c), bf16)
        gains = gains.at[0, :n_d].set(norm_attn).at[1, :n_d].set(norm_ffn)
        pack = jnp.concatenate([my_query, my_latent, my_key, my_value, my_out, gains], 0)
        cuts = [n_d, 2 * n_d, 2 * n_d + n_l, 2 * n_d + 2 * n_l, 3 * n_d + 2 * n_l]

        col = lax.broadcasted_iota(jnp.int32, (S * R * n_f, FFq), 1)
        row = lax.broadcasted_iota(jnp.int32, (S * R * n_f, FFq), 0)
        pick = (row == (col // n_f) * (R * n_f) + r * n_f + col % n_f).astype(bf16)
        my_gate_up = dot_nn(jnp.concatenate([w_gate, w_up], 0), pick).astype(bf16)
        my_down = lax.dynamic_slice_in_dim(w_down, r * n_f, n_f, 0)

        all_tokens = gather_rep(tokens).reshape(R * T, D)
        packs = gather_shard(pack)
        all_cot = gather_rep(cotangent).reshape(R * T, D)
        gate_up = gather_shard(my_gate_up)
        down = gather_shard(my_down).reshape(FFq, D)

        query_w = packs[:, : cuts[0]].reshape(D, q_c)
        latent_w = packs[:, cuts[0] : cuts[1]].reshape(D, LAT)
        key_w = packs[:, cuts[1] : cuts[2]].reshape(LAT, q_c)
        value_w = packs[:, cuts[2] : cuts[3]].reshape(LAT, q_c)
        out_w = packs[:, cuts[3] : cuts[4]].reshape(D, q_c)
        gain_attn = packs[:, cuts[4], :n_d].reshape(D).astype(f32)
        gain_ffn = packs[:, cuts[4] + 1, :n_d].reshape(D).astype(f32)
        gate_w = gate_up[:, :n_d].reshape(D, FFq)
        up_w = gate_up[:, n_d:].reshape(D, FFq)

        heads = q_c // HD
        group_in = all_tokens.astype(f32)
        scale_attn = rms_scale(group_in)
        normed_attn = (group_in * scale_attn * gain_attn).astype(bf16)
        queries = dot_nn(normed_attn, query_w).astype(bf16)
        latents = dot_nn(normed_attn, latent_w).astype(bf16)
        keys = dot_nn(latents, key_w).astype(bf16)
        values = dot_nn(latents, value_w).astype(bf16)
        qh = queries.reshape(R, T, heads, HD)
        kh = keys.reshape(R, T, heads, HD)
        vh = values.reshape(R, T, heads, HD)
        row_ids = lax.broadcasted_iota(jnp.int32, (SEQ, SEQ), 0)
        col_ids = lax.broadcasted_iota(jnp.int32, (SEQ, SEQ), 1)
        scores = jnp.einsum("bqhd,bkhd->bhqk", qh, kh, preferred_element_type=f32) * HD**-0.5
        scores = jnp.where(col_ids <= row_ids, scores, -1e30)
        maxima = jnp.max(scores, axis=-1, keepdims=True)
        exps = jnp.exp(scores - maxima)
        probs = exps / jnp.sum(exps, axis=-1, keepdims=True)
        low_probs = probs.astype(bf16)
        mixed = jnp.einsum("bhqk,bkhd->bqhd", low_probs, vh, preferred_element_type=f32)
        mixed = mixed.astype(bf16).reshape(R * T, q_c)
        attn_part = dot_nt(mixed, out_w).reshape(R, T, D)
        inputs = tokens.astype(f32)
        residual = inputs + scatter_rep(attn_part)
        scale_ffn = rms_scale(residual)
        normed_own = (residual * scale_ffn * gain_ffn).astype(bf16)
        normed_ffn = gather_rep(normed_own).reshape(R * T, D)

        gate_proj = dot_nn(normed_ffn, gate_w)
        up_proj = dot_nn(normed_ffn, up_w)
        sig = jax.nn.sigmoid(gate_proj)
        silu = gate_proj * sig
        activated = (silu * up_proj).astype(bf16)
        grad_down = dot_tn(activated, all_cot).astype(bf16).reshape(S, n_f, D)
        grad_act = dot_nt(all_cot, down)
        grad_gate = (grad_act * up_proj * sig * (1.0 + gate_proj * (1.0 - sig))).astype(bf16)
        grad_up = (grad_act * silu).astype(bf16)
        grad_gate_w = dot_tn(normed_ffn, grad_gate).astype(bf16).reshape(S, n_d, FFq)
        grad_up_w = dot_tn(normed_ffn, grad_up).astype(bf16).reshape(S, n_d, FFq)
        ffn_back = dot_nt(grad_gate, gate_w) + dot_nt(grad_up, up_w)
        grad_normed_ffn = scatter_rep(ffn_back.reshape(R, T, D))
        ffn_part = dot_nn(activated, down).reshape(R, T, D)
        output = (residual + scatter_rep(ffn_part)).astype(bf16)

        weighted = grad_normed_ffn * gain_ffn
        grad_residual = (
            cotangent.astype(f32)
            + scale_ffn * weighted
            - residual * scale_ffn**3 * jnp.mean(weighted * residual, axis=-1, keepdims=True)
        )
        grad_attn = gather_rep(grad_residual.astype(bf16)).reshape(R * T, D)

        grad_out_w = dot_tn(grad_attn, mixed).astype(bf16)
        grad_mixed = dot_nn(grad_attn, out_w).astype(bf16).reshape(R, T, heads, HD)
        grad_probs = jnp.einsum("bqhd,bkhd->bhqk", grad_mixed, vh, preferred_element_type=f32)
        grad_scores = (
            probs * (grad_probs - jnp.sum(probs * grad_probs, axis=-1, keepdims=True))
        ).astype(bf16)
        grad_q = jnp.einsum("bhqk,bkhd->bqhd", grad_scores, kh, preferred_element_type=f32)
        grad_k = jnp.einsum("bhqk,bqhd->bkhd", grad_scores, qh, preferred_element_type=f32)
        grad_v = jnp.einsum("bhqk,bqhd->bkhd", low_probs, grad_mixed, preferred_element_type=f32)
        grad_q = (grad_q * HD**-0.5).astype(bf16).reshape(R * T, q_c)
        grad_k = (grad_k * HD**-0.5).astype(bf16).reshape(R * T, q_c)
        grad_v = grad_v.astype(bf16).reshape(R * T, q_c)
        grad_key_w = dot_tn(latents, grad_k).astype(bf16)
        grad_value_w = dot_tn(latents, grad_v).astype(bf16)
        grad_query_w = dot_tn(normed_attn, grad_q).astype(bf16)
        lat_part = (dot_nt(grad_k, key_w) + dot_nt(grad_v, value_w)).reshape(R, T, LAT)
        near = flip_core(lat_part[1::2])
        grad_lat = (lat_part[0::2] + near).astype(bf16).reshape(2 * T, LAT)
        half_normed = normed_attn.reshape(R, T, D)[0::2].reshape(2 * T, D)
        grad_latent_w = dot_tn(half_normed, grad_lat).astype(bf16)
        attn_back = dot_nt(grad_q, query_w).reshape(R, T, D)
        lat_back = dot_nt(grad_lat, latent_w).reshape(2, T, D)
        attn_back = jnp.stack(
            [attn_back[0] + lat_back[0], attn_back[1], attn_back[2] + lat_back[1], attn_back[3]]
        )
        grad_normed_attn = scatter_rep(attn_back)
        weighted = grad_normed_attn * gain_attn
        scale_own = rms_scale(inputs)
        grad_tokens = (
            grad_residual
            + scale_own * weighted
            - inputs * scale_own**3 * jnp.mean(weighted * inputs, axis=-1, keepdims=True)
        ).astype(bf16)

        sum_down = scatter_shard(grad_down)
        sum_gate = scatter_shard(grad_gate_w)
        sum_up = scatter_shard(grad_up_w)
        grad_pack = jnp.concatenate(
            [
                grad_query_w.reshape(S, n_d, q_c),
                grad_latent_w.reshape(S, n_d, LAT),
                grad_key_w.reshape(S, n_l, q_c),
                grad_value_w.reshape(S, n_l, q_c),
                grad_out_w.reshape(S, n_d, q_c),
            ],
            1,
        )
        sum_pack = scatter_shard(grad_pack).astype(f32)
        g_query = sum_pack[:, : cuts[0]].transpose(1, 0, 2).reshape(n_d, R * q_c)
        g_latent = sum_pack[:, cuts[0] : cuts[1]]
        g_latent = jnp.concatenate([g_latent[0] + g_latent[1], g_latent[2] + g_latent[3]], 1)
        g_key = sum_pack[:, cuts[1] : cuts[2]].reshape(LG, 2, n_l, q_c)
        g_key = g_key.transpose(0, 2, 1, 3).reshape(LG, n_l, 2 * q_c)
        g_value = sum_pack[:, cuts[2] : cuts[3]].reshape(LG, 2, n_l, q_c)
        g_value = g_value.transpose(0, 2, 1, 3).reshape(LG, n_l, 2 * q_c)
        g_out = sum_pack[:, cuts[3] : cuts[4]].transpose(0, 2, 1).reshape(R * q_c, n_d)
        g_down = sum_down.reshape(R * n_f, D).astype(f32)

        def spread(v):
            v = v.reshape(R, n_d, S, n_f).transpose(1, 2, 0, 3)
            return v.reshape(n_d, S * R * n_f).astype(f32)

        g_gate = spread(sum_gate)
        g_up = spread(sum_up)
        g_norm_attn = (
            jnp.sum(g_query * w_query.astype(f32), axis=1)
            + jnp.sum(g_latent * w_latent.astype(f32), axis=1)
        ) / norm_attn.astype(f32)
        g_norm_ffn = (
            jnp.sum(g_gate * w_gate.astype(f32), axis=1) + jnp.sum(g_up * w_up.astype(f32), axis=1)
        ) / norm_ffn.astype(f32)
        return (
            output,
            grad_tokens,
            g_norm_attn,
            g_query,
            g_latent,
            g_key,
            g_value,
            g_out,
            g_norm_ffn,
            g_gate,
            g_up,
            g_down,
        )

    return layer


def solution(mesh):
    return jax.shard_map(
        make_layer(mesh),
        mesh=mesh,
        in_specs=(
            P(("rep", "shard"), None),
            P("shard"),
            P("shard", None),
            P("shard", None),
            P(None, "shard", None),
            P(None, "shard", None),
            P(None, "shard"),
            P("shard"),
            P("shard", None),
            P("shard", None),
            P("shard", None),
            P(("rep", "shard"), None),
        ),
        out_specs=(
            P(("rep", "shard"), None),
            P(("rep", "shard"), None),
            P("shard"),
            P("shard", None),
            P("shard", None),
            P(None, "shard", None),
            P(None, "shard", None),
            P(None, "shard"),
            P("shard"),
            P("shard", None),
            P("shard", None),
            P("shard", None),
        ),
        check_vma=False,
    )
```

time: 1530 us -> 480 us (0.31)
  waiting for transfers between devices: 1240 us -> 144 us
  local copies, waits for them, and re-layouts: 7.24 us -> 156 us
  blocking collectives: 129 us -> 0 us
  starting transfers between devices: 0.82 us -> 71.4 us
  matrix products: 95.8 us -> 56.1 us
    reduce_scatter x8 -> x0, waiting for transfers between devices: 912 us -> none  [the longest x1 194 us: shards(): lax.psum_scatter(grad_w_gate, 'shard', scatter_dimension=0, tiled=True)]
    all_gather x6 -> x0, waiting for transfers between devices: 299 us -> none  [the longest x1 90.3 us: shards(): lax.all_gather(w_gate, 'shard', axis=0, tiled=True)]
    ppermute x0 -> x62, waiting for transfers between devices: none -> 144 us  [the longest x16 56.7 us: flip_y(): return lax.ppermute(v, 'shard', [(i, i ^ 1) for i in range(S)])]
    all_gather x4 -> x0, blocking collectives: 103 us -> none  [the longest x1 32.4 us: shards(): lax.all_gather(w_key_up, 'shard', axis=1, tiled=True)]
    ppermute x0 -> x62, starting transfers between devices: none -> 71.4 us  [the longest x21 33.8 us: rot_z(): return lax.ppermute(v, 'shard', [(i, (i + 2 * k) % S) for i in range(S)])]
    dynamic_update_slice x0 -> x25, local copies, waits for them, and re-layouts: none -> 44.8 us  [the longest x12 24.6 us: gather_shard(): lax.dynamic_update_slice(full, other[None, None], (at, 1 - y) + zeros)]
    dot_general x30, matrix products: 95.8 us -> 51.4 us  [the longest x9 21.4 us: dot_nn(): lax.dot_general(a, b, (((1,), (0,)), ((), ())), preferred_element_type=f32)]
    psum x1 -> x0, waiting for transfers between devices: 26.6 us -> none  [shards(): lax.psum(group_sums[1].astype(jnp.bfloat16), 'rep').astype(jnp.float32)]
  transfers between devices with their start and end apart: 15 -> 62, of which waited for: 13 -> 24; matrix products, arithmetic and copies ran while one was open for 6% -> 40% of each run, Pallas kernels for 0% -> 0%
where the time goes in v1:
time: 480 us; the launch traced here: 472 us
  local copies, waits for them, and re-layouts  156 us (32%)
  waiting for transfers between devices  144 us (30%)
  starting transfers between devices  71.4 us (15%)
  matrix products  56.1 us (12%)
  other arithmetic  42.1 us (9%)
    ppermute x16, waiting for transfers between devices, flip_y(): return lax.ppermute(v, 'shard', [(i, i ^ 1) for i in range(S)])  56.7 us
    ppermute x21, waiting for transfers between devices, rot_z(): return lax.ppermute(v, 'shard', [(i, (i + 2 * k) % S) for i in range(S)])  52.4 us
    ppermute x12, waiting for transfers between devices, flip_x(): return lax.ppermute(v, 'rep', [(i, i ^ 2) for i in range(R)])  34.4 us
    ppermute x21, starting transfers between devices, rot_z(): return lax.ppermute(v, 'shard', [(i, (i + 2 * k) % S) for i in range(S)])  33.8 us
    dynamic_update_slice x12, local copies, waits for them, and re-layouts, gather_shard(): lax.dynamic_update_slice(full, other[None, None], (at, 1 - y) + zeros)  24.6 us
    unnamed x201, local copies, waits for them, and re-layouts  23.1 us
    dot_general x9, matrix products, dot_nn(): lax.dot_general(a, b, (((1,), (0,)), ((), ())), preferred_element_type=f32)  21.4 us
    dynamic_update_slice x13, local copies, waits for them, and re-layouts, gather_shard(): full = lax.dynamic_update_slice(full, piece[None, None], (at, y) + zeros)  20.2 us
  transfers between devices with their start and end apart: 62, of which 24 were waited for; matrix products, arithmetic and copies ran while one was open for 40% of the time, Pallas kernels for 0%

profile of v1, /device:TPU:0, one launch (start us, length us, event | category | flops | bytes accessed | tf_op | source)
XLA Modules:
  0.0 471.7 jit_solution(13935129322202013522)
XLA Ops:
  5.9 3.0 collective-permute-start.2
  23.4 4.5 bitcast_dynamic-update-slice_fusion.6
  32.4 5.3 %collective-permute-done.21 = bf16[88,1024]{1,0:T(8,128)(2,1)S(1)} collective-permute-done((bf16[88,1024]{1,0:T(8,128)(2,1)}, bf16[88,1024]{1,0:T(8,128)(2,1)S(1)}, u32[]{:S(2)}, u32[]{:S(2)}) %collective-permute-start.21) | collective-permute-done | bytes 180256 | tf_op jit(solution)/shard_map/ppermute | solution.py:48
  45.9 5.8 %collective-permute-done.4 = bf16[464,256]{0,1:T(8,128)(2,1)S(1)} collective-permute-done((bf16[464,256]{0,1:T(8,128)(2,1)}, bf16[464,256]{0,1:T(8,128)(2,1)S(1)}, u32[]{:S(2)}, u32[]{:S(2)}) %collective-permute-start.4) | collective-permute-done | bytes 237600 | tf_op jit(solution)/shard_map/ppermute | solution.py:45
  63.3 4.1 copy.295
  72.0 2.6 fusion.103
  75.4 4.6 collective-permute-done.23
  85.6 4.0 copy.297
  93.9 2.8 reshape.584
  98.8 3.2 convolution_convert_fusion.10
  102.0 2.8 reshape.585
  109.1 2.8 reshape.586
  114.0 4.7 fusion.114
  118.8 2.9 convolution_convert_fusion.9
  125.9 3.5 collective-permute-start.25
  131.0 3.2 collective-permute-done.25
  134.2 4.4 collective-permute-start.18
  155.2 8.5 %collective-permute-done.10 = bf16[256,1024]{1,0:T(8,128)(2,1)S(1)} collective-permute-done((bf16[256,1024]{1,0:T(8,128)(2,1)S(1)}, bf16[256,1024]{1,0:T(8,128)(2,1)S(1)}, u32[]{:S(2)}, u32[]{:S(2)}) %collective-permute-start.10) | collective-permute-done | bytes 524320 | tf_op jit(solution)/shard_map/ppermute | solution.py:42
  167.0 9.6 %collective-permute-done.11 = bf16[256,1024]{1,0:T(8,128)(2,1)S(1)} collective-permute-done((bf16[256,1024]{1,0:T(8,128)(2,1)S(1)}, bf16[256,1024]{1,0:T(8,128)(2,1)S(1)}, u32[]{:S(2)}, u32[]{:S(2)}) %collective-permute-start.11) | collective-permute-done | bytes 524320 | tf_op jit(solution)/shard_map/ppermute | solution.py:42
  177.7 4.6 copy.306
  182.9 14.2 %dynamic_update_slice.87 = bf16[4,2,256,704]{2,1,0,3:T(2,128)(2,1)} dynamic-update-slice(bf16[4,2,256,704]{2,1,0,3:T(2,128)(2,1)} %copy.306, bf16[1,1,256,704]{2,1,0,3:T(2,128)(2,1)S(1)} %copy.307, s32[]{:T(128)S(6)} %select_n.251, s32[]{:T(128)S(6)} %select_n.248, s32[]{:T(128)} %constant.262.clone.1, s32[]{:T(128)} %constant.262.clone.1) | dynamic-update-slice | bytes 720900 | tf_op jit(solution)/shard_map/dynamic_update_slice | solution.py:97
  197.1 7.0 %reshape.485 = bf16[8,256,704]{1,0,2:T(8,128)(2,1)} reshape(bf16[4,2,256,704]{2,1,0,3:T(2,128)(2,1)} %dynamic_update_slice.87) | data formatting | bytes 5767168 | tf_op jit(solution)/shard_map/reshape | solution.py:98
  214.9 5.6 %multiply_convert_fusion.1 = (bf16[1024,704]{0,1:T(8,128)(2,1)S(1)}, bf16[1024,704]{0,1:T(8,128)(2,1)S(1)}, bf16[1024,704]{0,1:T(8,128)(2,1)}) fusion(f32[1024,704]{0,1:T(8,128)S(1)} %fusion.24, f32[1024,704]{0,1:T(8,128)S(1)} %fusion.20, bf16[1024,1024]{1,0:T(8,128)(2,1)S(1)} %bitcast.459, bf16[704,1024]{1,0:T(8,128)(2,1)} %bitcast.48), kind=kOutput, calls=%fused_computation.30 | convolution fusion | flops 1487208448 | bytes 13631488 | tf_op jit(solution)/shard_map/dot_general | solution.py:26
  222.3 2.8 convolution_convert_fusion.1
  225.1 2.8 convolution_convert_fusion
  233.3 3.8 reshape_reshape.13
  237.1 4.1 constant_dynamic-slice_fusion.3
  243.2 3.9 reshape_reshape.14
  247.2 3.0 constant_dynamic-slice_fusion.1
  254.6 3.2 fusion.116
  258.0 3.5 collective-permute-done.44
  263.1 13.7 %collective-permute-done.50 = bf16[4,128,704]{1,2,0:T(8,128)(2,1)S(1)} collective-permute-done((bf16[4,128,704]{1,2,0:T(8,128)(2,1)S(1)}, bf16[4,128,704]{1,2,0:T(8,128)(2,1)S(1)}, u32[]{:S(2)}, u32[]{:S(2)}) %collective-permute-start.50) | collective-permute-done | bytes 720928 | tf_op jit(solution)/shard_map/ppermute | solution.py:45
  277.0 14.3 %collective-permute-done.56 = bf16[4,88,1024]{2,1,0:T(8,128)(2,1)S(1)} collective-permute-done((bf16[4,88,1024]{2,1,0:T(8,128)(2,1)S(1)}, bf16[4,88,1024]{2,1,0:T(8,128)(2,1)S(1)}, u32[]{:S(2)}, u32[]{:S(2)}) %collective-permute-start.56) | collective-permute-done | bytes 720928 | tf_op jit(solution)/shard_map/ppermute | solution.py:45
  291.7 3.9 collective-permute-start.53
  295.6 5.0 %collective-permute-done.45 = bf16[128,704]{0,1:T(8,128)(2,1)S(1)} collective-permute-done((bf16[128,704]{0,1:T(8,128)(2,1)S(1)}, bf16[128,704]{0,1:T(8,128)(2,1)S(1)}, u32[]{:S(2)}, u32[]{:S(2)}) %collective-permute-start.45) | collective-permute-done | bytes 180256 | tf_op jit(solution)/shard_map/ppermute | solution.py:48
  300.7 3.1 collective-permute-done.53
  305.0 7.6 %collective-permute-done.52 = bf16[128,704]{0,1:T(8,128)(2,1)S(1)} collective-permute-done((bf16[128,704]{0,1:T(8,128)(2,1)S(1)}, bf16[128,704]{0,1:T(8,128)(2,1)S(1)}, u32[]{:S(2)}, u32[]{:S(2)}) %collective-permute-start.52) | collective-permute-done | bytes 180256 | tf_op jit(solution)/shard_map/ppermute | solution.py:48
  312.5 7.2 %collective-permute-start.57 = (bf16[88,1024]{1,0:T(8,128)(2,1)S(1)}, bf16[88,1024]{1,0:T(8,128)(2,1)S(1)}, u32[]{:S(2)}, u32[]{:S(2)}) collective-permute-start(bf16[88,1024]{1,0:T(8,128)(2,1)S(1)} %get-tuple-element.132), channel_id=1, source_target_pairs={{0,2},{1,3},{2,4},{3,5},{4,6},{5,7},{6,0},{7,1},{8,10},{9,11},{10,... | collective-permute-start | bytes 540680 | tf_op jit(solution)/shard_map/ppermute | solution.py:48
  321.4 5.6 %collective-permute-done.58 = bf16[88,1024]{1,0:T(8,128)(2,1)S(1)} collective-permute-done((bf16[88,1024]{1,0:T(8,128)(2,1)S(1)}, bf16[88,1024]{1,0:T(8,128)(2,1)S(1)}, u32[]{:S(2)}, u32[]{:S(2)}) %collective-permute-start.58) | collective-permute-done | bytes 180256 | tf_op jit(solution)/shard_map/ppermute | solution.py:48
  341.0 2.6 gather_fusion.2
  347.9 2.6 gather_fusion.4
  350.5 2.6 gather_fusion.3
  354.6 4.7 collective-permute-done.28
  359.3 3.1 fusion.101
  367.3 7.5 %collective-permute-done.33 = bf16[256,1024]{1,0:T(8,128)(2,1)S(1)} collective-permute-done((bf16[256,1024]{1,0:T(8,128)(2,1)}, bf16[256,1024]{1,0:T(8,128)(2,1)S(1)}, u32[]{:S(2)}, u32[]{:S(2)}) %collective-permute-start.33) | collective-permute-done | bytes 524320 | tf_op jit(solution)/shard_map/ppermute | solution.py:42
  389.3 3.3 multiply_reduce_fusion
  411.1 18.1 %collective-permute-done.38 = bf16[4,448,256]{2,1,0:T(8,128)(2,1)S(1)} collective-permute-done((bf16[4,448,256]{2,1,0:T(8,128)(2,1)S(1)}, bf16[4,448,256]{2,1,0:T(8,128)(2,1)S(1)}, u32[]{:S(2)}, u32[]{:S(2)}) %collective-permute-start.38) | collective-permute-done | bytes 917536 | tf_op jit(solution)/shard_map/ppermute | solution.py:45
  437.8 12.9 %collective-permute-done.40 = bf16[448,256]{1,0:T(8,128)(2,1)S(1)} collective-permute-done((bf16[448,256]{1,0:T(8,128)(2,1)S(1)}, bf16[448,256]{1,0:T(8,128)(2,1)S(1)}, u32[]{:S(2)}, u32[]{:S(2)}) %collective-permute-start.40) | collective-permute-done | bytes 229408 | tf_op jit(solution)/shard_map/ppermute | solution.py:48
  (478 shorter events, 210.2 us)
Async XLA Ops:
  5.9 34.0 %collective-permute-start.2 = (bf16[464,256]{0,1:T(8,128)(2,1)S(1)}, bf16[464,256]{0,1:T(8,128)(2,1)}, u32[]{:S(2)}, u32[]{:S(2)}) collective-permute-start(bf16[464,256]{0,1:T(8,128)(2,1)S(1)} %concatenate.29), channel_id=1, source_target_pairs={{0,1},{1,0},{2,3},{3,2},{4,5},{5,4},{6,7},{7,6},{8,9},{9,8},{10,11... | collective-permute-start | bytes 712712 | tf_op jit(solution)/shard_map/ppermute | solution.py:45
  9.0 31.1 %collective-permute-start.3 = (bf16[464,256]{0,1:T(8,128)(2,1)S(1)}, bf16[464,256]{0,1:T(8,128)(2,1)}, u32[]{:S(2)}, u32[]{:S(2)}) collective-permute-start(bf16[464,256]{0,1:T(8,128)(2,1)S(1)} %concatenate.29), channel_id=1, source_target_pairs={{0,2},{1,3},{2,4},{3,5},{4,6},{5,7},{6,0},{7,1},{8,10},{9,11},{10,... | collective-permute-start | bytes 712712 | tf_op jit(solution)/shard_map/ppermute | solution.py:48
  10.5 33.9 %collective-permute-start.5 = (bf16[464,256]{0,1:T(8,128)(2,1)S(1)}, bf16[464,256]{0,1:T(8,128)(2,1)}, u32[]{:S(2)}, u32[]{:S(2)}) collective-permute-start(bf16[464,256]{0,1:T(8,128)(2,1)S(1)} %concatenate.29), channel_id=1, source_target_pairs={{0,4},{1,5},{2,6},{3,7},{4,0},{5,1},{6,2},{7,3},{8,12},{9,13},{10,... | collective-permute-start | bytes 712712 | tf_op jit(solution)/shard_map/ppermute | solution.py:48
  13.1 42.5 %collective-permute-start.7 = (bf16[464,256]{0,1:T(8,128)(2,1)S(1)}, bf16[464,256]{0,1:T(8,128)(2,1)S(1)}, u32[]{:S(2)}, u32[]{:S(2)}) collective-permute-start(bf16[464,256]{0,1:T(8,128)(2,1)S(1)} %concatenate.29), channel_id=1, source_target_pairs={{0,6},{1,7},{2,0},{3,1},{4,2},{5,3},{6,4},{7,5},{8,14},{9,15},{10,... | collective-permute-start | bytes 712712 | tf_op jit(solution)/shard_map/ppermute | solution.py:48
  17.5 12.6 %collective-permute-start.20 = (bf16[88,1024]{1,0:T(8,128)(2,1)}, bf16[88,1024]{1,0:T(8,128)(2,1)}, u32[]{:S(2)}, u32[]{:S(2)}) collective-permute-start(bf16[88,1024]{1,0:T(8,128)(2,1)} %get-tuple-element.93), channel_id=1, source_target_pairs={{0,1},{1,0},{2,3},{3,2},{4,5},{5,4},{6,7},{7,6},{8,9},{9,8},{10,11... | collective-permute-start | bytes 540680 | tf_op jit(solution)/shard_map/ppermute | solution.py:45
  37.7 101.6 %collective-permute-start.13 = (bf16[256,704]{0,1:T(8,128)(2,1)}, bf16[256,704]{0,1:T(8,128)(2,1)}, u32[]{:S(2)}, u32[]{:S(2)}) collective-permute-start(bf16[256,704]{0,1:T(8,128)(2,1)} %get-tuple-element.158), channel_id=1, source_target_pairs={{0,1},{1,0},{2,3},{3,2},{4,5},{5,4},{6,7},{7,6},{8,9},{9,8},{10,11... | collective-permute-start | bytes 1081352 | tf_op jit(solution)/shard_map/ppermute | solution.py:45
  39.9 101.9 %collective-permute-start.14 = (bf16[256,704]{0,1:T(8,128)(2,1)}, bf16[256,704]{0,1:T(8,128)(2,1)}, u32[]{:S(2)}, u32[]{:S(2)}) collective-permute-start(bf16[256,704]{0,1:T(8,128)(2,1)} %get-tuple-element.158), channel_id=1, source_target_pairs={{0,2},{1,3},{2,4},{3,5},{4,6},{5,7},{6,0},{7,1},{8,10},{9,11},{10,... | collective-permute-start | bytes 1081352 | tf_op jit(solution)/shard_map/ppermute | solution.py:48
  40.1 11.7 %collective-permute-start.4 = (bf16[464,256]{0,1:T(8,128)(2,1)}, bf16[464,256]{0,1:T(8,128)(2,1)S(1)}, u32[]{:S(2)}, u32[]{:S(2)}) collective-permute-start(bf16[464,256]{0,1:T(8,128)(2,1)} %collective-permute-done.3), channel_id=1, source_target_pairs={{0,1},{1,0},{2,3},{3,2},{4,5},{5,4},{6,7},{7,6},{8,9},{9,8},{10,11... | collective-permute-start | bytes 712712 | tf_op jit(solution)/shard_map/ppermute | solution.py:45
  44.5 17.0 %collective-permute-start = (bf16[256,1024]{0,1:T(8,128)(2,1)S(1)}, bf16[256,1024]{0,1:T(8,128)(2,1)S(1)}, u32[]{:S(2)}, u32[]{:S(2)}) collective-permute-start(bf16[256,1024]{0,1:T(8,128)(2,1)S(1)} %copy-done.14), channel_id=1, source_target_pairs={{0,16},{8,24},{16,0},{24,8},{1,17},{9,25},{17,1},{25,9},{2,18},{10... | collective-permute-start | bytes 1572872 | tf_op jit(solution)/shard_map/ppermute | solution.py:42
  55.7 87.2 %collective-permute-start.16 = (bf16[256,704]{0,1:T(8,128)(2,1)}, bf16[256,704]{0,1:T(8,128)(2,1)}, u32[]{:S(2)}, u32[]{:S(2)}) collective-permute-start(bf16[256,704]{0,1:T(8,128)(2,1)} %get-tuple-element.158), channel_id=1, source_target_pairs={{0,4},{1,5},{2,6},{3,7},{4,0},{5,1},{6,2},{7,3},{8,12},{9,13},{10,... | collective-permute-start | bytes 1081352 | tf_op jit(solution)/shard_map/ppermute | solution.py:48
  62.6 18.5 %collective-permute-start.1 = (bf16[2,256,1024]{1,2,0:T(8,128)(2,1)}, bf16[2,256,1024]{1,2,0:T(8,128)(2,1)}, u32[]{:S(2)}, u32[]{:S(2)}) collective-permute-start(bf16[2,256,1024]{1,2,0:T(8,128)(2,1)} %pad_maximum_fusion.5), channel_id=1, source_target_pairs={{0,8},{8,0},{16,24},{24,16},{1,9},{9,1},{17,25},{25,17},{2,10},{10... | collective-permute-start | bytes 3145736 | tf_op jit(solution)/shard_map/ppermute | solution.py:39
  67.4 12.5 %collective-permute-start.23 = (bf16[88,1024]{1,0:T(8,128)(2,1)}, bf16[88,1024]{1,0:T(8,128)(2,1)}, u32[]{:S(2)}, u32[]{:S(2)}) collective-permute-start(bf16[88,1024]{1,0:T(8,128)(2,1)} %get-tuple-element.93), channel_id=1, source_target_pairs={{0,4},{1,5},{2,6},{3,7},{4,0},{5,1},{6,2},{7,3},{8,12},{9,13},{10,... | collective-permute-start | bytes 540680 | tf_op jit(solution)/shard_map/ppermute | solution.py:48
  80.0 42.6 %collective-permute-start.22 = (bf16[88,1024]{1,0:T(8,128)(2,1)S(1)}, bf16[88,1024]{1,0:T(8,128)(2,1)}, u32[]{:S(2)}, u32[]{:S(2)}) collective-permute-start(bf16[88,1024]{1,0:T(8,128)(2,1)S(1)} %copy-done.83), channel_id=1, source_target_pairs={{0,1},{1,0},{2,3},{3,2},{4,5},{5,4},{6,7},{7,6},{8,9},{9,8},{10,11... | collective-permute-start | bytes 540680 | tf_op jit(solution)/shard_map/ppermute | solution.py:45
  81.0 44.8 %collective-permute-start.24 = (bf16[88,1024]{1,0:T(8,128)(2,1)}, bf16[88,1024]{1,0:T(8,128)(2,1)}, u32[]{:S(2)}, u32[]{:S(2)}) collective-permute-start(bf16[88,1024]{1,0:T(8,128)(2,1)} %collective-permute-done.23), channel_id=1, source_target_pairs={{0,1},{1,0},{2,3},{3,2},{4,5},{5,4},{6,7},{7,6},{8,9},{9,8},{10,11... | collective-permute-start | bytes 540680 | tf_op jit(solution)/shard_map/ppermute | solution.py:45
  122.6 24.9 %collective-permute-start.9 = (bf16[2,256,1024]{2,1,0:T(8,128)(2,1)S(1)}, bf16[2,256,1024]{2,1,0:T(8,128)(2,1)S(1)}, u32[]{:S(2)}, u32[]{:S(2)}) collective-permute-start(bf16[2,256,1024]{2,1,0:T(8,128)(2,1)S(1)} %slice.241), channel_id=1, source_target_pairs={{0,8},{8,0},{16,24},{24,16},{1,9},{9,1},{17,25},{25,17},{2,10},{10... | collective-permute-start | bytes 3145736 | tf_op jit(solution)/shard_map/ppermute | solution.py:39
  134.2 12.2 %collective-permute-start.18 = (bf16[256,704]{0,1:T(8,128)(2,1)}, bf16[256,704]{0,1:T(8,128)(2,1)S(1)}, u32[]{:S(2)}, u32[]{:S(2)}) collective-permute-start(bf16[256,704]{0,1:T(8,128)(2,1)} %get-tuple-element.158), channel_id=1, source_target_pairs={{0,6},{1,7},{2,0},{3,1},{4,2},{5,3},{6,4},{7,5},{8,14},{9,15},{10,... | collective-permute-start | bytes 1081352 | tf_op jit(solution)/shard_map/ppermute | solution.py:48
  139.2 14.9 %collective-permute-start.29 = (bf16[256,1024]{1,0:T(8,128)(2,1)S(1)}, bf16[256,1024]{1,0:T(8,128)(2,1)S(1)}, u32[]{:S(2)}, u32[]{:S(2)}) collective-permute-start(bf16[256,1024]{1,0:T(8,128)(2,1)S(1)} %copy-done.22), channel_id=1, source_target_pairs={{0,16},{8,24},{16,0},{24,8},{1,17},{9,25},{17,1},{25,9},{2,18},{10... | collective-permute-start | bytes 1572872 | tf_op jit(solution)/shard_map/ppermute | solution.py:42
  142.9 22.9 %collective-permute-start.15 = (bf16[256,704]{0,1:T(8,128)(2,1)}, bf16[256,704]{0,1:T(8,128)(2,1)S(1)}, u32[]{:S(2)}, u32[]{:S(2)}) collective-permute-start(bf16[256,704]{0,1:T(8,128)(2,1)} %collective-permute-done.14), channel_id=1, source_target_pairs={{0,1},{1,0},{2,3},{3,2},{4,5},{5,4},{6,7},{7,6},{8,9},{9,8},{10,11... | collective-permute-start | bytes 1081352 | tf_op jit(solution)/shard_map/ppermute | solution.py:45
  146.4 31.3 %collective-permute-start.17 = (bf16[256,704]{0,1:T(8,128)(2,1)}, bf16[256,704]{0,1:T(8,128)(2,1)S(1)}, u32[]{:S(2)}, u32[]{:S(2)}) collective-permute-start(bf16[256,704]{0,1:T(8,128)(2,1)} %collective-permute-done.16), channel_id=1, source_target_pairs={{0,1},{1,0},{2,3},{3,2},{4,5},{5,4},{6,7},{7,6},{8,9},{9,8},{10,11... | collective-permute-start | bytes 1081352 | tf_op jit(solution)/shard_map/ppermute | solution.py:45
  147.5 34.9 %collective-permute-start.19 = (bf16[256,704]{0,1:T(8,128)(2,1)S(1)}, bf16[256,704]{0,1:T(8,128)(2,1)S(1)}, u32[]{:S(2)}, u32[]{:S(2)}) collective-permute-start(bf16[256,704]{0,1:T(8,128)(2,1)S(1)} %collective-permute-done.18), channel_id=1, source_target_pairs={{0,1},{1,0},{2,3},{3,2},{4,5},{5,4},{6,7},{7,6},{8,9},{9,8},{10,11... | collective-permute-start | bytes 1081352 | tf_op jit(solution)/shard_map/ppermute | solution.py:45
  149.3 14.4 %collective-permute-start.10 = (bf16[256,1024]{1,0:T(8,128)(2,1)S(1)}, bf16[256,1024]{1,0:T(8,128)(2,1)S(1)}, u32[]{:S(2)}, u32[]{:S(2)}) collective-permute-start(bf16[256,1024]{1,0:T(8,128)(2,1)S(1)} %fusion.70), channel_id=1, source_target_pairs={{0,16},{8,24},{16,0},{24,8},{1,17},{9,25},{17,1},{25,9},{2,18},{10... | collective-permute-start | bytes 1572872 | tf_op jit(solution)/shard_map/ppermute | solution.py:42
  155.2 52.3 %collective-permute-start.30 = (bf16[2,256,1024]{2,1,0:T(8,128)(2,1)}, bf16[2,256,1024]{2,1,0:T(8,128)(2,1)}, u32[]{:S(2)}, u32[]{:S(2)}) collective-permute-start(bf16[2,256,1024]{2,1,0:T(8,128)(2,1)} %pad_maximum_fusion.7), channel_id=1, source_target_pairs={{0,8},{8,0},{16,24},{24,16},{1,9},{9,1},{17,25},{25,17},{2,10},{10... | collective-permute-start | bytes 3145736 | tf_op jit(solution)/shard_map/ppermute | solution.py:39
  164.2 12.4 %collective-permute-start.11 = (bf16[256,1024]{1,0:T(8,128)(2,1)S(1)}, bf16[256,1024]{1,0:T(8,128)(2,1)S(1)}, u32[]{:S(2)}, u32[]{:S(2)}) collective-permute-start(bf16[256,1024]{1,0:T(8,128)(2,1)S(1)} %multiply_convert_fusion.4), channel_id=1, source_target_pairs={{0,16},{8,24},{16,0},{24,8},{1,17},{9,25},{17,1},{25,9},{2,18},{10... | collective-permute-start | bytes 1572872 | tf_op jit(solution)/shard_map/ppermute | solution.py:42
  177.7 31.5 %collective-permute-start.12 = (bf16[2,256,1024]{2,1,0:T(8,128)(2,1)}, bf16[2,256,1024]{2,1,0:T(8,128)(2,1)}, u32[]{:S(2)}, u32[]{:S(2)}) collective-permute-start(bf16[2,256,1024]{2,1,0:T(8,128)(2,1)} %pad_maximum_fusion.6), channel_id=1, source_target_pairs={{0,8},{8,0},{16,24},{24,16},{1,9},{9,1},{17,25},{25,17},{2,10},{10... | collective-permute-start | bytes 3145736 | tf_op jit(solution)/shard_map/ppermute | solution.py:39
  232.8 96.5 %collective-permute-start.31 = (bf16[2,256,1024]{2,1,0:T(8,128)(2,1)}, bf16[2,256,1024]{2,1,0:T(8,128)(2,1)}, u32[]{:S(2)}, u32[]{:S(2)}) collective-permute-start(bf16[2,256,1024]{2,1,0:T(8,128)(2,1)} %slice.256), channel_id=1, source_target_pairs={{0,8},{8,0},{16,24},{24,16},{1,9},{9,1},{17,25},{25,17},{2,10},{10... | collective-permute-start | bytes 3145736 | tf_op jit(solution)/shard_map/ppermute | solution.py:39
  242.2 19.3 %collective-permute-start.44 = (bf16[4,128,704]{1,2,0:T(8,128)(2,1)}, bf16[4,128,704]{1,2,0:T(8,128)(2,1)}, u32[]{:S(2)}, u32[]{:S(2)}) collective-permute-start(bf16[4,128,704]{1,2,0:T(8,128)(2,1)} %bitcast.386), channel_id=1, source_target_pairs={{0,1},{1,0},{2,3},{3,2},{4,5},{5,4},{6,7},{7,6},{8,9},{9,8},{10,11... | collective-permute-start | bytes 2162696 | tf_op jit(solution)/shard_map/ppermute | solution.py:45
  250.3 26.5 %collective-permute-start.50 = (bf16[4,128,704]{1,2,0:T(8,128)(2,1)S(1)}, bf16[4,128,704]{1,2,0:T(8,128)(2,1)S(1)}, u32[]{:S(2)}, u32[]{:S(2)}) collective-permute-start(bf16[4,128,704]{1,2,0:T(8,128)(2,1)S(1)} %bitcast.492), channel_id=1, source_target_pairs={{0,1},{1,0},{2,3},{3,2},{4,5},{5,4},{6,7},{7,6},{8,9},{9,8},{10,11... | collective-permute-start | bytes 2162696 | tf_op jit(solution)/shard_map/ppermute | solution.py:45
  253.5 37.8 %collective-permute-start.56 = (bf16[4,88,1024]{2,1,0:T(8,128)(2,1)S(1)}, bf16[4,88,1024]{2,1,0:T(8,128)(2,1)S(1)}, u32[]{:S(2)}, u32[]{:S(2)}) collective-permute-start(bf16[4,88,1024]{2,1,0:T(8,128)(2,1)S(1)} %dynamic-slice_bitcast_fusion.1), channel_id=1, source_target_pairs={{0,1},{1,0},{2,3},{3,2},{4,5},{5,4},{6,7},{7,6},{8,9},{9,8},{10,11... | collective-permute-start | bytes 2162696 | tf_op jit(solution)/shard_map/ppermute | solution.py:45
  257.9 75.3 %collective-permute-start.27 = (bf16[2,256,1024]{2,1,0:T(8,128)(2,1)S(1)}, bf16[2,256,1024]{2,1,0:T(8,128)(2,1)S(1)}, u32[]{:S(2)}, u32[]{:S(2)}) collective-permute-start(bf16[2,256,1024]{2,1,0:T(8,128)(2,1)S(1)} %slice.250), channel_id=1, source_target_pairs={{0,8},{8,0},{16,24},{24,16},{1,9},{9,1},{17,25},{25,17},{2,10},{10... | collective-permute-start | bytes 3145736 | tf_op jit(solution)/shard_map/ppermute | solution.py:39
  262.8 28.9 %collective-permute-start.47 = (bf16[128,704]{0,1:T(8,128)(2,1)S(1)}, bf16[128,704]{0,1:T(8,128)(2,1)S(1)}, u32[]{:S(2)}, u32[]{:S(2)}) collective-permute-start(bf16[128,704]{0,1:T(8,128)(2,1)S(1)} %get-tuple-element.139), channel_id=1, source_target_pairs={{0,6},{1,7},{2,0},{3,1},{4,2},{5,3},{6,4},{7,5},{8,14},{9,15},{10,... | collective-permute-start | bytes 540680 | tf_op jit(solution)/shard_map/ppermute | solution.py:48
  276.8 18.8 %collective-permute-start.46 = (bf16[128,704]{0,1:T(8,128)(2,1)S(1)}, bf16[128,704]{0,1:T(8,128)(2,1)S(1)}, u32[]{:S(2)}, u32[]{:S(2)}) collective-permute-start(bf16[128,704]{0,1:T(8,128)(2,1)S(1)} %get-tuple-element.140), channel_id=1, source_target_pairs={{0,4},{1,5},{2,6},{3,7},{4,0},{5,1},{6,2},{7,3},{8,12},{9,13},{10,... | collective-permute-start | bytes 540680 | tf_op jit(solution)/shard_map/ppermute | solution.py:48
  291.7 12.1 %collective-permute-start.53 = (bf16[128,704]{0,1:T(8,128)(2,1)S(1)}, bf16[128,704]{0,1:T(8,128)(2,1)S(1)}, u32[]{:S(2)}, u32[]{:S(2)}) collective-permute-start(bf16[128,704]{0,1:T(8,128)(2,1)S(1)} %get-tuple-element.136), channel_id=1, source_target_pairs={{0,6},{1,7},{2,0},{3,1},{4,2},{5,3},{6,4},{7,5},{8,14},{9,15},{10,... | collective-permute-start | bytes 540680 | tf_op jit(solution)/shard_map/ppermute | solution.py:48
  295.6 16.9 %collective-permute-start.52 = (bf16[128,704]{0,1:T(8,128)(2,1)S(1)}, bf16[128,704]{0,1:T(8,128)(2,1)S(1)}, u32[]{:S(2)}, u32[]{:S(2)}) collective-permute-start(bf16[128,704]{0,1:T(8,128)(2,1)S(1)} %get-tuple-element.137), channel_id=1, source_target_pairs={{0,4},{1,5},{2,6},{3,7},{4,0},{5,1},{6,2},{7,3},{8,12},{9,13},{10,... | collective-permute-start | bytes 540680 | tf_op jit(solution)/shard_map/ppermute | solution.py:48
  300.6 11.9 %collective-permute-start.51 = (bf16[128,704]{0,1:T(8,128)(2,1)S(1)}, bf16[128,704]{0,1:T(8,128)(2,1)S(1)}, u32[]{:S(2)}, u32[]{:S(2)}) collective-permute-start(bf16[128,704]{0,1:T(8,128)(2,1)S(1)} %get-tuple-element.135), channel_id=1, source_target_pairs={{0,2},{1,3},{2,4},{3,5},{4,6},{5,7},{6,0},{7,1},{8,10},{9,11},{10,... | collective-permute-start | bytes 540680 | tf_op jit(solution)/shard_map/ppermute | solution.py:48
  303.8 16.0 %collective-permute-start.59 = (bf16[88,1024]{1,0:T(8,128)(2,1)S(1)}, bf16[88,1024]{1,0:T(8,128)(2,1)S(1)}, u32[]{:S(2)}, u32[]{:S(2)}) collective-permute-start(bf16[88,1024]{1,0:T(8,128)(2,1)S(1)} %get-tuple-element.133), channel_id=1, source_target_pairs={{0,6},{1,7},{2,0},{3,1},{4,2},{5,3},{6,4},{7,5},{8,14},{9,15},{10,... | collective-permute-start | bytes 540680 | tf_op jit(solution)/shard_map/ppermute | solution.py:48
  312.5 14.6 %collective-permute-start.58 = (bf16[88,1024]{1,0:T(8,128)(2,1)S(1)}, bf16[88,1024]{1,0:T(8,128)(2,1)S(1)}, u32[]{:S(2)}, u32[]{:S(2)}) collective-permute-start(bf16[88,1024]{1,0:T(8,128)(2,1)S(1)} %get-tuple-element.134), channel_id=1, source_target_pairs={{0,4},{1,5},{2,6},{3,7},{4,0},{5,1},{6,2},{7,3},{8,12},{9,13},{10,... | collective-permute-start | bytes 540680 | tf_op jit(solution)/shard_map/ppermute | solution.py:48
  312.5 16.0 %collective-permute-start.57 = (bf16[88,1024]{1,0:T(8,128)(2,1)S(1)}, bf16[88,1024]{1,0:T(8,128)(2,1)S(1)}, u32[]{:S(2)}, u32[]{:S(2)}) collective-permute-start(bf16[88,1024]{1,0:T(8,128)(2,1)S(1)} %get-tuple-element.132), channel_id=1, source_target_pairs={{0,2},{1,3},{2,4},{3,5},{4,6},{5,7},{6,0},{7,1},{8,10},{9,11},{10,... | collective-permute-start | bytes 540680 | tf_op jit(solution)/shard_map/ppermute | solution.py:48
  319.9 13.7 %collective-permute-start.48 = (bf16[128,704]{0,1:T(8,128)(2,1)S(1)}, bf16[128,704]{0,1:T(8,128)(2,1)S(1)}, u32[]{:S(2)}, u32[]{:S(2)}) collective-permute-start(bf16[128,704]{0,1:T(8,128)(2,1)S(1)} %fusion.87), channel_id=1, source_target_pairs={{0,16},{8,24},{16,0},{24,8},{1,17},{9,25},{17,1},{25,9},{2,18},{10... | collective-permute-start | bytes 540680 | tf_op jit(solution)/shard_map/ppermute | solution.py:42
  328.7 9.7 %collective-permute-start.60 = (bf16[88,1024]{1,0:T(8,128)(2,1)S(1)}, bf16[88,1024]{1,0:T(8,128)(2,1)S(1)}, u32[]{:S(2)}, u32[]{:S(2)}) collective-permute-start(bf16[88,1024]{1,0:T(8,128)(2,1)S(1)} %fusion.81), channel_id=1, source_target_pairs={{0,16},{8,24},{16,0},{24,8},{1,17},{9,25},{17,1},{25,9},{2,18},{10... | collective-permute-start | bytes 540680 | tf_op jit(solution)/shard_map/ppermute | solution.py:42
  331.7 21.4 %collective-permute-start.32 = (bf16[256,1024]{1,0:T(8,128)(2,1)}, bf16[256,1024]{1,0:T(8,128)(2,1)}, u32[]{:S(2)}, u32[]{:S(2)}) collective-permute-start(bf16[256,1024]{1,0:T(8,128)(2,1)} %fusion.72), channel_id=1, source_target_pairs={{0,16},{8,24},{16,0},{24,8},{1,17},{9,25},{17,1},{25,9},{2,18},{10... | collective-permute-start | bytes 1572872 | tf_op jit(solution)/shard_map/ppermute | solution.py:42
  335.8 23.4 %collective-permute-start.28 = (bf16[256,1024]{1,0:T(8,128)(2,1)}, bf16[256,1024]{1,0:T(8,128)(2,1)}, u32[]{:S(2)}, u32[]{:S(2)}) collective-permute-start(bf16[256,1024]{1,0:T(8,128)(2,1)} %fusion.71), channel_id=1, source_target_pairs={{0,16},{8,24},{16,0},{24,8},{1,17},{9,25},{17,1},{25,9},{2,18},{10... | collective-permute-start | bytes 1572872 | tf_op jit(solution)/shard_map/ppermute | solution.py:42
  339.2 26.3 %collective-permute-start.61 = (bf16[2,88,1024]{2,1,0:T(8,128)(2,1)}, bf16[2,88,1024]{2,1,0:T(8,128)(2,1)}, u32[]{:S(2)}, u32[]{:S(2)}) collective-permute-start(bf16[2,88,1024]{2,1,0:T(8,128)(2,1)} %pad_maximum_fusion.16), channel_id=1, source_target_pairs={{0,8},{8,0},{16,24},{24,16},{1,9},{9,1},{17,25},{25,17},{2,10},{10... | collective-permute-start | bytes 1081352 | tf_op jit(solution)/shard_map/ppermute | solution.py:39
  362.4 12.4 %collective-permute-start.33 = (bf16[256,1024]{1,0:T(8,128)(2,1)}, bf16[256,1024]{1,0:T(8,128)(2,1)S(1)}, u32[]{:S(2)}, u32[]{:S(2)}) collective-permute-start(bf16[256,1024]{1,0:T(8,128)(2,1)} %get-tuple-element.88), channel_id=1, source_target_pairs={{0,16},{8,24},{16,0},{24,8},{1,17},{9,25},{17,1},{25,9},{2,18},{10... | collective-permute-start | bytes 1572872 | tf_op jit(solution)/shard_map/ppermute | solution.py:42
  406.4 22.8 %collective-permute-start.38 = (bf16[4,448,256]{2,1,0:T(8,128)(2,1)S(1)}, bf16[4,448,256]{2,1,0:T(8,128)(2,1)S(1)}, u32[]{:S(2)}, u32[]{:S(2)}) collective-permute-start(bf16[4,448,256]{2,1,0:T(8,128)(2,1)S(1)} %dynamic-slice_bitcast_fusion), channel_id=1, source_target_pairs={{0,1},{1,0},{2,3},{3,2},{4,5},{5,4},{6,7},{7,6},{8,9},{9,8},{10,11... | collective-permute-start | bytes 2752520 | tf_op jit(solution)/shard_map/ppermute | solution.py:45
  409.2 23.4 %collective-permute-start.36 = (bf16[2,256,1024]{2,1,0:T(8,128)(2,1)S(1)}, bf16[2,256,1024]{2,1,0:T(8,128)(2,1)S(1)}, u32[]{:S(2)}, u32[]{:S(2)}) collective-permute-start(bf16[2,256,1024]{2,1,0:T(8,128)(2,1)S(1)} %slice.272), channel_id=1, source_target_pairs={{0,8},{8,0},{16,24},{24,16},{1,9},{9,1},{17,25},{25,17},{2,10},{10... | collective-permute-start | bytes 3145736 | tf_op jit(solution)/shard_map/ppermute | solution.py:39
  429.6 21.1 %collective-permute-start.40 = (bf16[448,256]{1,0:T(8,128)(2,1)S(1)}, bf16[448,256]{1,0:T(8,128)(2,1)S(1)}, u32[]{:S(2)}, u32[]{:S(2)}) collective-permute-start(bf16[448,256]{1,0:T(8,128)(2,1)S(1)} %get-tuple-element.131), channel_id=1, source_target_pairs={{0,4},{1,5},{2,6},{3,7},{4,0},{5,1},{6,2},{7,3},{8,12},{9,13},{10,... | collective-permute-start | bytes 688136 | tf_op jit(solution)/shard_map/ppermute | solution.py:48
  430.8 19.9 %collective-permute-start.39 = (bf16[448,256]{1,0:T(8,128)(2,1)S(1)}, bf16[448,256]{1,0:T(8,128)(2,1)S(1)}, u32[]{:S(2)}, u32[]{:S(2)}) collective-permute-start(bf16[448,256]{1,0:T(8,128)(2,1)S(1)} %get-tuple-element.129), channel_id=1, source_target_pairs={{0,2},{1,3},{2,4},{3,5},{4,6},{5,7},{6,0},{7,1},{8,10},{9,11},{10,... | collective-permute-start | bytes 688136 | tf_op jit(solution)/shard_map/ppermute | solution.py:48
  433.8 23.6 %collective-permute-start.37 = (bf16[256,1024]{1,0:T(8,128)(2,1)}, bf16[256,1024]{1,0:T(8,128)(2,1)}, u32[]{:S(2)}, u32[]{:S(2)}) collective-permute-start(bf16[256,1024]{1,0:T(8,128)(2,1)} %fusion.73), channel_id=1, source_target_pairs={{0,16},{8,24},{16,0},{24,8},{1,17},{9,25},{17,1},{25,9},{2,18},{10... | collective-permute-start | bytes 1572872 | tf_op jit(solution)/shard_map/ppermute | solution.py:42
  (106 other events, 642.7 us)
